TPU v7x, 32 devices: a whole 2x2x4 slice. The times are simulated.
32 devices in a mesh: runs: 2 (over y), shot: 4 (over x, core), slab: 4 (over z).
Axes of the slice: x: 2, y: 2, z: 4, core: 2. Of those that a mesh axis runs over, the one named last changes fastest.
Arguments:
- source_now: float32 [16, 64, 16, 256], P(('runs', 'shot'), 'slab'), parts along dimension 0, may hold values from -4 to 4
- source_prev: float32 [16, 64, 16, 256], P(('runs', 'shot'), 'slab'), parts along dimension 0, may hold values from -4 to 4
- receiver_now: float32 [16, 64, 16, 256], P(('runs', 'shot'), 'slab'), parts along dimension 0, may hold values from -4 to 4
- receiver_prev: float32 [16, 64, 16, 256], P(('runs', 'shot'), 'slab'), parts along dimension 0, may hold values from -4 to 4
- courant_sq: float32 [128, 16, 256], P(('runs', 'slab')), parts along dimension 0, may hold values from 0.26 to 0.52
- source_cell: int32 [16], P(('runs', 'shot')), parts along dimension 0, may hold values from 0 to 1023
- wavelet: float32 [8, 16], P(None, ('runs', 'shot')), parts along dimension 1, may hold values from -12 to 12
- receiver_cell: int32 [16, 256], P(('runs', 'shot')), parts along dimension 0, may hold values from 0 to 1023
- traces: float32 [8, 16, 256], P(None, ('runs', 'shot')), parts along dimension 1, may hold values from -10 to 10
- offset_perm: int32 [16], P('runs'), parts along dimension 0, may hold values from 0 to 7, each once
Outputs:
- offset_image: float32 [16, 64, 16, 256], P(('runs', 'shot'), 'slab'), parts along dimension 0
- source_final: float32 [16, 64, 16, 256], P(('runs', 'shot'), 'slab'), parts along dimension 0
- receiver_final: float32 [16, 64, 16, 256], P(('runs', 'shot'), 'slab'), parts along dimension 0
There are 2 independent parts, one for each index of `runs`. A program takes and returns all parts, laid end to end along the dimension named above; each array names one. Nothing has to cross between parts.
Inputs may be any that keep to these rules, and one draw needn't show every extreme that they name: `source_cell`: a surface cell index. `receiver_cell`: surface cell indices; two receivers may share a cell. `offset_perm`: every offset index appears once.
All inputs are finite; a program needn't handle non-finite values.
Results may differ from a plain program's by a relative error of at most 0.0003.
Values sent between devices are 32-bit elements; how exact they have to be, the bound alone decides.
A program may use at most 64 MiB of HBM per device.

v0:
```python
import jax
import jax.numpy as jnp
from jax import lax
from jax.sharding import PartitionSpec as P

OFF_DEV = 2
STEPS = 8
INJECT_Z = 4


stencil_weights = (-205.0 / 72.0, 8.0 / 5.0, -1.0 / 5.0, 8.0 / 315.0, -1.0 / 560.0)
side_weight = 1.0 / 16.0


def extended_2(cells, sides, width):
    for axis, dim in sides:
        count = lax.axis_size(axis)
        ends = count - 1
        head = lax.slice_in_dim(cells, 0, width, axis=dim)
        tail = lax.slice_in_dim(cells, cells.shape[dim] - width, cells.shape[dim], axis=dim)
        cells = jnp.concatenate(
            [
                lax.ppermute(tail, axis, [(i, (i + 1) % count) for i in range(ends)]),
                cells,
                lax.ppermute(head, axis, [((i + 1) % count, i) for i in range(ends)]),
            ],
            axis=dim,
        )
    return cells


def laplace_rows(extended):
    row_count = extended.shape[2] - 8
    centre = extended[:, :, 4 : 4 + row_count]
    size_y = centre.shape[3]
    size_z = centre.shape[4]
    padded = jnp.pad(centre, ((0, 0), (0, 0), (0, 0), (4, 4), (4, 4)))
    summed = (1.0 + 2.0 * side_weight) * stencil_weights[0] * centre
    for distance in range(1, 5):
        weight = stencil_weights[distance]
        summed = summed + weight * (
            extended[:, :, 4 + distance : 4 + distance + row_count]
            + extended[:, :, 4 - distance : 4 - distance + row_count]
        )
        summed = summed + side_weight * weight * (
            padded[:, :, :, 4 + distance : 4 + distance + size_y, 4 : 4 + size_z]
            + padded[:, :, :, 4 - distance : 4 - distance + size_y, 4 : 4 + size_z]
        )
        summed = summed + side_weight * weight * (
            padded[:, :, :, 4 : 4 + size_y, 4 + distance : 4 + distance + size_z]
            + padded[:, :, :, 4 : 4 + size_y, 4 - distance : 4 - distance + size_z]
        )
    return summed


def hot_tables(source_cell, receiver_cell, first_row, row_count, cells_y):
    positions = lax.broadcasted_iota(jnp.int32, (1, row_count * cells_y), 1) + first_row * cells_y
    source_hot = (source_cell[:, None] == positions).astype(jnp.float32)
    receiver_hot = (receiver_cell[:, :, None] == positions[None]).astype(jnp.float32)
    return (source_hot, receiver_hot)


def correlate(source_pad, receiver_pad, shift_by, half_span, extent):
    shifted_source = lax.dynamic_slice_in_dim(source_pad, half_span - shift_by, extent, axis=2)
    shifted_receiver = lax.dynamic_slice_in_dim(receiver_pad, half_span + shift_by, extent, axis=2)
    return jnp.sum(shifted_source * shifted_receiver, axis=0)


def body(
    source_now,
    source_prev,
    receiver_now,
    receiver_prev,
    courant_sq,
    source_cell,
    wavelet,
    receiver_cell,
    traces,
    offset_perm,
):
    shots_here, rows_here, cells_y, cells_z = source_now.shape
    slab_start = lax.axis_index("slab") * rows_here
    grid_rows = rows_here * lax.axis_size("slab")
    fields = jnp.stack([source_now, receiver_now])
    before = jnp.stack([source_prev, receiver_prev])
    local_tables = hot_tables(source_cell, receiver_cell, slab_start, rows_here, cells_y)
    for moment in range(STEPS):
        extended = extended_2(fields, (("slab", 2),), 4)
        row_count = extended.shape[2] - 8
        centre = extended[:, :, 4 : 4 + row_count]
        updated = 2.0 * centre - before + courant_sq * laplace_rows(extended)
        source_hot, receiver_hot = local_tables
        source_plane = source_hot * wavelet[moment][:, None]
        receiver_plane = jnp.einsum(
            "sr,src->sc", traces[moment], receiver_hot, precision=lax.Precision.HIGHEST
        )
        planes = jnp.stack([source_plane, receiver_plane]).reshape(
            2, shots_here, row_count, cells_y
        )
        updated = updated.at[:, :, :, :, INJECT_Z].add(planes)
        global_rows = slab_start + lax.broadcasted_iota(jnp.int32, (row_count,), 0)
        inside = (global_rows >= 0) & (global_rows < grid_rows)
        updated = jnp.where(inside[None, None, :, None, None], updated, 0.0)
        before, fields = (fields, updated)
    half_span = offset_perm.shape[0] // 2
    pad_widths = ((0, 0), (0, 0), (half_span, half_span), (0, 0))
    own_lags = lax.dynamic_slice_in_dim(offset_perm, lax.axis_index("shot") * OFF_DEV, OFF_DEV)
    shard_piece = lax.all_gather(fields, "shot", axis=1, tiled=True)
    source_pad = jnp.pad(shard_piece[0], pad_widths)
    receiver_pad = jnp.pad(shard_piece[1], pad_widths)
    products = [
        correlate(source_pad, receiver_pad, own_lags[slot_index] - half_span, half_span, cells_y)
        for slot_index in range(OFF_DEV)
    ]
    offset_image = jnp.stack(products)
    return (offset_image, fields[0], fields[1])


def solution(mesh):
    in_specs = (
        P(("runs", "shot"), "slab", None, None),
        P(("runs", "shot"), "slab", None, None),
        P(("runs", "shot"), "slab", None, None),
        P(("runs", "shot"), "slab", None, None),
        P(("runs", "slab"), None, None),
        P(("runs", "shot")),
        P(None, ("runs", "shot")),
        P(("runs", "shot"), None),
        P(None, ("runs", "shot"), None),
        P("runs"),
    )
    out_specs = (
        P(("runs", "shot"), "slab", None, None),
        P(("runs", "shot"), "slab", None, None),
        P(("runs", "shot"), "slab", None, None),
    )
    return jax.shard_map(body, mesh=mesh, in_specs=in_specs, out_specs=out_specs, check_vma=False)
```

profile of v0, /device:TPU:0, one launch (start us, length us, event | category | flops | bytes accessed | tf_op | source)
XLA Modules:
  0.0 271.8 jit_solution(146948616227826346)
XLA Ops:
  9.9 5.6 %collective-permute-start.1 = (f32[2,2,4,16,256]{4,3,2,1,0:T(8,128)S(1)}, f32[2,2,4,16,256]{4,3,2,1,0:T(8,128)S(1)}, u32[]{:S(2)}, u32[]{:S(2)}) collective-permute-start(f32[2,2,4,16,256]{4,3,2,1,0:T(8,128)S(1)} %get-tuple-element.139), channel_id=1, source_target_pairs={{0,1},{1,2},{2,3},{4,5},{5,6},{6,7},{8,9},{9,10},{10,11},{12,13},{... | collective-permute-start | bytes 786440 | tf_op jit(solution)/shard_map/ppermute | solution.py:23
  25.1 5.3 %scatter-add.26 = f32[2,2,16,16,256]{4,3,2,1,0:T(8,128)S(1)} dynamic-update-slice(f32[2,2,16,16,256]{4,3,2,1,0:T(8,128)S(1)} %fusion.216, f32[2,2,16,16,1]{4,3,2,1,0:T(8,128)S(1)} %copy.241, s32[]{:T(128)} %constant.214.clone.1, s32[]{:T(128)} %constant.214.clone.1, s32[]{:T(128)} %constant.214.clone.1, s32[]{:T(128)} %constant.214.clone.1, s32[]{:T(128)} %constant.228.clone.1) | dynamic-update-slice | bytes 8196 | tf_op jit(solution)/shard_map/scatter-add | solution.py:100
  32.9 5.7 %collective-permute-start.3 = (f32[2,2,4,16,256]{4,3,2,1,0:T(8,128)S(1)}, f32[2,2,4,16,256]{4,3,2,1,0:T(8,128)}, u32[]{:S(2)}, u32[]{:S(2)}) collective-permute-start(f32[2,2,4,16,256]{4,3,2,1,0:T(8,128)S(1)} %get-tuple-element.135), channel_id=1, source_target_pairs={{0,1},{1,2},{2,3},{4,5},{5,6},{6,7},{8,9},{9,10},{10,11},{12,13},{... | collective-permute-start | bytes 786440 | tf_op jit(solution)/shard_map/ppermute | solution.py:23
  42.6 14.2 %fusion.186 = f32[2,2,16,16,256]{4,3,2,1,0:T(8,128)S(1)} fusion(f32[2,2,16,16,256]{4,3,2,1,0:T(8,128)} %copy-done.10, f32[2,2,4,16,256]{4,3,2,1,0:T(8,128)} %collective-permute-done.3, f32[2,2,4,16,256]{4,3,2,1,0:T(8,128)} %copy-done.13, f32[16,16,256]{2,1,0:T(8,128)S(1)} %copy-done, f32[1,2,16,16,256]{4,3,2,1,0:T(8,128)S(1)} %bitcast.77, ...), kind=kLoop, calls=%fused_computation.411 | loop fusion | flops 13107200 | bytes 3932160 | tf_op jit(solution)/shard_map/add | solution.py:91
  58.0 6.7 %scatter-add.29 = f32[2,2,16,16,256]{4,3,2,1,0:T(8,128)} dynamic-update-slice(f32[2,2,16,16,256]{4,3,2,1,0:T(8,128)} %copy-done.5, f32[2,2,16,16,1]{4,3,2,1,0:T(8,128)S(1)} %copy.244, s32[]{:T(128)} %constant.214.clone.1, s32[]{:T(128)} %constant.214.clone.1, s32[]{:T(128)} %constant.214.clone.1, s32[]{:T(128)} %constant.214.clone.1, s32[]{:T(128)} %constant.228.clone.1) | dynamic-update-slice | bytes 8196 | tf_op jit(solution)/shard_map/scatter-add | solution.py:100
  67.5 5.1 %collective-permute-start.5 = (f32[2,2,4,16,256]{4,3,2,1,0:T(8,128)S(1)}, f32[2,2,4,16,256]{4,3,2,1,0:T(8,128)S(1)}, u32[]{:S(2)}, u32[]{:S(2)}) collective-permute-start(f32[2,2,4,16,256]{4,3,2,1,0:T(8,128)S(1)} %get-tuple-element.133), channel_id=1, source_target_pairs={{0,1},{1,2},{2,3},{4,5},{5,6},{6,7},{8,9},{9,10},{10,11},{12,13},{... | collective-permute-start | bytes 786440 | tf_op jit(solution)/shard_map/ppermute | solution.py:23
  76.5 4.5 %fusion.160 = f32[2,2,16,16,256]{4,3,2,1,0:T(8,128)} fusion(f32[2,2,16,16,256]{4,3,2,1,0:T(8,128)S(1)} %broadcast_select_fusion.6, f32[2,2,4,16,256]{4,3,2,1,0:T(8,128)S(1)} %collective-permute-done.5, f32[2,2,4,16,256]{4,3,2,1,0:T(8,128)S(1)} %collective-permute-done.4, f32[16,16,256]{2,1,0:T(8,128)S(1)} %copy-done, ...), kind=kLoop, calls=%fused_computation.385 | loop fusion | flops 13107200 | bytes 3932176 | tf_op jit(solution)/shard_map/add | solution.py:91
  83.1 6.7 %scatter-add.30 = f32[2,2,16,16,256]{4,3,2,1,0:T(8,128)} dynamic-update-slice(f32[2,2,16,16,256]{4,3,2,1,0:T(8,128)} %fusion.160, f32[2,2,16,16,1]{4,3,2,1,0:T(8,128)S(1)} %copy.247, s32[]{:T(128)} %constant.214.clone.1, s32[]{:T(128)} %constant.214.clone.1, s32[]{:T(128)} %constant.214.clone.1, s32[]{:T(128)} %constant.214.clone.1, s32[]{:T(128)} %constant.228.clone.1) | dynamic-update-slice | bytes 8196 | tf_op jit(solution)/shard_map/scatter-add | solution.py:100
  92.6 5.2 %collective-permute-start.7 = (f32[2,2,4,16,256]{4,3,2,1,0:T(8,128)S(1)}, f32[2,2,4,16,256]{4,3,2,1,0:T(8,128)S(1)}, u32[]{:S(2)}, u32[]{:S(2)}) collective-permute-start(f32[2,2,4,16,256]{4,3,2,1,0:T(8,128)S(1)} %get-tuple-element.131), channel_id=1, source_target_pairs={{0,1},{1,2},{2,3},{4,5},{5,6},{6,7},{8,9},{9,10},{10,11},{12,13},{... | collective-permute-start | bytes 786440 | tf_op jit(solution)/shard_map/ppermute | solution.py:23
  101.5 4.5 %fusion.134 = f32[2,2,16,16,256]{4,3,2,1,0:T(8,128)} fusion(f32[2,2,16,16,256]{4,3,2,1,0:T(8,128)S(1)} %broadcast_select_fusion.5, f32[2,2,4,16,256]{4,3,2,1,0:T(8,128)S(1)} %collective-permute-done.7, f32[2,2,4,16,256]{4,3,2,1,0:T(8,128)S(1)} %collective-permute-done.6, f32[16,16,256]{2,1,0:T(8,128)S(1)} %copy-done, ...), kind=kLoop, calls=%fused_computation.359 | loop fusion | flops 13107200 | bytes 3932176 | tf_op jit(solution)/shard_map/add | solution.py:91
  108.1 6.7 %scatter-add.31 = f32[2,2,16,16,256]{4,3,2,1,0:T(8,128)} dynamic-update-slice(f32[2,2,16,16,256]{4,3,2,1,0:T(8,128)} %fusion.134, f32[2,2,16,16,1]{4,3,2,1,0:T(8,128)S(1)} %copy.250, s32[]{:T(128)} %constant.214.clone.1, s32[]{:T(128)} %constant.214.clone.1, s32[]{:T(128)} %constant.214.clone.1, s32[]{:T(128)} %constant.214.clone.1, s32[]{:T(128)} %constant.228.clone.1) | dynamic-update-slice | bytes 8196 | tf_op jit(solution)/shard_map/scatter-add | solution.py:100
  117.7 5.0 %collective-permute-start.9 = (f32[2,2,4,16,256]{4,3,2,1,0:T(8,128)S(1)}, f32[2,2,4,16,256]{4,3,2,1,0:T(8,128)S(1)}, u32[]{:S(2)}, u32[]{:S(2)}) collective-permute-start(f32[2,2,4,16,256]{4,3,2,1,0:T(8,128)S(1)} %get-tuple-element.129), channel_id=1, source_target_pairs={{0,1},{1,2},{2,3},{4,5},{5,6},{6,7},{8,9},{9,10},{10,11},{12,13},{... | collective-permute-start | bytes 786440 | tf_op jit(solution)/shard_map/ppermute | solution.py:23
  126.6 4.5 %fusion.108 = f32[2,2,16,16,256]{4,3,2,1,0:T(8,128)} fusion(f32[2,2,16,16,256]{4,3,2,1,0:T(8,128)S(1)} %broadcast_select_fusion.4, f32[2,2,4,16,256]{4,3,2,1,0:T(8,128)S(1)} %collective-permute-done.9, f32[2,2,4,16,256]{4,3,2,1,0:T(8,128)S(1)} %collective-permute-done.8, f32[16,16,256]{2,1,0:T(8,128)S(1)} %copy-done, ...), kind=kLoop, calls=%fused_computation.333 | loop fusion | flops 13107200 | bytes 3932176 | tf_op jit(solution)/shard_map/add | solution.py:91
  133.2 6.7 %scatter-add.34 = f32[2,2,16,16,256]{4,3,2,1,0:T(8,128)} dynamic-update-slice(f32[2,2,16,16,256]{4,3,2,1,0:T(8,128)} %fusion.108, f32[2,2,16,16,1]{4,3,2,1,0:T(8,128)S(1)} %copy.253, s32[]{:T(128)} %constant.214.clone.1, s32[]{:T(128)} %constant.214.clone.1, s32[]{:T(128)} %constant.214.clone.1, s32[]{:T(128)} %constant.214.clone.1, s32[]{:T(128)} %constant.228.clone.1) | dynamic-update-slice | bytes 8196 | tf_op jit(solution)/shard_map/scatter-add | solution.py:100
  142.7 5.0 %collective-permute-start.11 = (f32[2,2,4,16,256]{4,3,2,1,0:T(8,128)S(1)}, f32[2,2,4,16,256]{4,3,2,1,0:T(8,128)S(1)}, u32[]{:S(2)}, u32[]{:S(2)}) collective-permute-start(f32[2,2,4,16,256]{4,3,2,1,0:T(8,128)S(1)} %get-tuple-element.127), channel_id=1, source_target_pairs={{0,1},{1,2},{2,3},{4,5},{5,6},{6,7},{8,9},{9,10},{10,11},{12,13},{... | collective-permute-start | bytes 786440 | tf_op jit(solution)/shard_map/ppermute | solution.py:23
  151.6 4.5 %fusion.82 = f32[2,2,16,16,256]{4,3,2,1,0:T(8,128)} fusion(f32[2,2,16,16,256]{4,3,2,1,0:T(8,128)S(1)} %broadcast_select_fusion.3, f32[2,2,4,16,256]{4,3,2,1,0:T(8,128)S(1)} %collective-permute-done.11, f32[2,2,4,16,256]{4,3,2,1,0:T(8,128)S(1)} %collective-permute-done.10, f32[16,16,256]{2,1,0:T(8,128)S(1)} %copy-done, ...), kind=kLoop, calls=%fused_computation.307 | loop fusion | flops 13107200 | bytes 3932176 | tf_op jit(solution)/shard_map/add | solution.py:91
  158.2 6.7 %scatter-add.35 = f32[2,2,16,16,256]{4,3,2,1,0:T(8,128)} dynamic-update-slice(f32[2,2,16,16,256]{4,3,2,1,0:T(8,128)} %fusion.82, f32[2,2,16,16,1]{4,3,2,1,0:T(8,128)S(1)} %copy.256, s32[]{:T(128)} %constant.214.clone.1, s32[]{:T(128)} %constant.214.clone.1, s32[]{:T(128)} %constant.214.clone.1, s32[]{:T(128)} %constant.214.clone.1, s32[]{:T(128)} %constant.228.clone.1) | dynamic-update-slice | bytes 8196 | tf_op jit(solution)/shard_map/scatter-add | solution.py:100
  167.8 5.3 %collective-permute-start.13 = (f32[2,2,4,16,256]{4,3,2,1,0:T(8,128)S(1)}, f32[2,2,4,16,256]{4,3,2,1,0:T(8,128)S(1)}, u32[]{:S(2)}, u32[]{:S(2)}) collective-permute-start(f32[2,2,4,16,256]{4,3,2,1,0:T(8,128)S(1)} %get-tuple-element.125), channel_id=1, source_target_pairs={{0,1},{1,2},{2,3},{4,5},{5,6},{6,7},{8,9},{9,10},{10,11},{12,13},{... | collective-permute-start | bytes 786440 | tf_op jit(solution)/shard_map/ppermute | solution.py:23
  176.7 4.5 %fusion.56 = f32[2,2,16,16,256]{4,3,2,1,0:T(8,128)} fusion(f32[2,2,16,16,256]{4,3,2,1,0:T(8,128)S(1)} %broadcast_select_fusion.2, f32[2,2,4,16,256]{4,3,2,1,0:T(8,128)S(1)} %collective-permute-done.13, f32[2,2,4,16,256]{4,3,2,1,0:T(8,128)S(1)} %collective-permute-done.12, f32[16,16,256]{2,1,0:T(8,128)S(1)} %copy-done, ...), kind=kLoop, calls=%fused_computation.281 | loop fusion | flops 13107200 | bytes 3932176 | tf_op jit(solution)/shard_map/add | solution.py:91
  183.3 6.7 %scatter-add.36 = f32[2,2,16,16,256]{4,3,2,1,0:T(8,128)} dynamic-update-slice(f32[2,2,16,16,256]{4,3,2,1,0:T(8,128)} %fusion.56, f32[2,2,16,16,1]{4,3,2,1,0:T(8,128)S(1)} %copy.259, s32[]{:T(128)} %constant.214.clone.1, s32[]{:T(128)} %constant.214.clone.1, s32[]{:T(128)} %constant.214.clone.1, s32[]{:T(128)} %constant.214.clone.1, s32[]{:T(128)} %constant.228.clone.1) | dynamic-update-slice | bytes 8196 | tf_op jit(solution)/shard_map/scatter-add | solution.py:100
  192.8 5.0 %collective-permute-start.15 = (f32[2,2,4,16,256]{4,3,2,1,0:T(8,128)S(1)}, f32[2,2,4,16,256]{4,3,2,1,0:T(8,128)S(1)}, u32[]{:S(2)}, u32[]{:S(2)}) collective-permute-start(f32[2,2,4,16,256]{4,3,2,1,0:T(8,128)S(1)} %get-tuple-element.123), channel_id=1, source_target_pairs={{0,1},{1,2},{2,3},{4,5},{5,6},{6,7},{8,9},{9,10},{10,11},{12,13},{... | collective-permute-start | bytes 786440 | tf_op jit(solution)/shard_map/ppermute | solution.py:23
  201.7 4.5 %fusion.30 = f32[2,2,16,16,256]{4,3,2,1,0:T(8,128)} fusion(f32[2,2,16,16,256]{4,3,2,1,0:T(8,128)S(1)} %broadcast_select_fusion.1, f32[2,2,4,16,256]{4,3,2,1,0:T(8,128)S(1)} %collective-permute-done.15, f32[2,2,4,16,256]{4,3,2,1,0:T(8,128)S(1)} %collective-permute-done.14, f32[16,16,256]{2,1,0:T(8,128)S(1)} %copy-done, ...), kind=kLoop, calls=%fused_computation.255 | loop fusion | flops 13107200 | bytes 3932176 | tf_op jit(solution)/shard_map/add | solution.py:91
  208.3 6.7 %scatter-add.39 = f32[2,2,16,16,256]{4,3,2,1,0:T(8,128)} dynamic-update-slice(f32[2,2,16,16,256]{4,3,2,1,0:T(8,128)} %fusion.30, f32[2,2,16,16,1]{4,3,2,1,0:T(8,128)S(1)} %copy.262, s32[]{:T(128)} %constant.214.clone.1, s32[]{:T(128)} %constant.214.clone.1, s32[]{:T(128)} %constant.214.clone.1, s32[]{:T(128)} %constant.214.clone.1, s32[]{:T(128)} %constant.228.clone.1) | dynamic-update-slice | bytes 8196 | tf_op jit(solution)/shard_map/scatter-add | solution.py:100
  224.4 30.6 %all-gather.2.cloned.1.call-done = f32[2,8,16,16,256]{4,3,2,1,0:T(8,128)} async-done(((f32[2,2,16,16,256]{4,3,2,1,0:T(8,128)}), f32[2,8,16,16,256]{4,3,2,1,0:T(8,128)}) %all-gather.2.cloned.1.call-update) | async-done | bytes 4194320 | tf_op jit(solution)/shard_map/all_gather | solution.py:108
  (175 shorter events, 85.8 us)
Async XLA Ops:
  7.2 8.4 %copy-start.9 = (f32[2,16,16,256]{3,2,1,0:T(8,128)S(1)}, f32[2,16,16,256]{3,2,1,0:T(8,128)}, u32[]{:S(2)}) copy-start(f32[2,16,16,256]{3,2,1,0:T(8,128)} %param.26) | copy-start | bytes 1572868
  7.2 247.8 %all-gather.2.cloned.1.call-start = ((), (), s32[]{:S(2)}) async-start(), calls=%async_computation | async-start | bytes 5242880 | tf_op jit(solution)/shard_map/all_gather | solution.py:108
  8.5 9.1 %copy-start.21 = (s32[2]{0:T(128)S(1)}, s32[2]{0:T(128)}, u32[]{:S(2)}) copy-start(s32[2]{0:T(128)} %param.31) | copy-start | bytes 28
  8.5 11.4 %collective-permute-start = (f32[2,2,4,16,256]{4,3,2,1,0:T(8,128)S(1)}, f32[2,2,4,16,256]{4,3,2,1,0:T(8,128)S(1)}, u32[]{:S(2)}, u32[]{:S(2)}) collective-permute-start(f32[2,2,4,16,256]{4,3,2,1,0:T(8,128)S(1)} %get-tuple-element.138), channel_id=1, source_target_pairs={{1,0},{2,1},{3,2},{5,4},{6,5},{7,6},{9,8},{10,9},{11,10},{13,12},{... | collective-permute-start | bytes 786440 | tf_op jit(solution)/shard_map/ppermute | solution.py:25
  9.9 11.1 %collective-permute-start.1 = (f32[2,2,4,16,256]{4,3,2,1,0:T(8,128)S(1)}, f32[2,2,4,16,256]{4,3,2,1,0:T(8,128)S(1)}, u32[]{:S(2)}, u32[]{:S(2)}) collective-permute-start(f32[2,2,4,16,256]{4,3,2,1,0:T(8,128)S(1)} %get-tuple-element.139), channel_id=1, source_target_pairs={{0,1},{1,2},{2,3},{4,5},{5,6},{6,7},{8,9},{9,10},{10,11},{12,13},{... | collective-permute-start | bytes 786440 | tf_op jit(solution)/shard_map/ppermute | solution.py:23
  31.6 9.8 %collective-permute-start.2 = (f32[2,2,4,16,256]{4,3,2,1,0:T(8,128)S(1)}, f32[2,2,4,16,256]{4,3,2,1,0:T(8,128)S(1)}, u32[]{:S(2)}, u32[]{:S(2)}) collective-permute-start(f32[2,2,4,16,256]{4,3,2,1,0:T(8,128)S(1)} %get-tuple-element.134), channel_id=1, source_target_pairs={{1,0},{2,1},{3,2},{5,4},{6,5},{7,6},{9,8},{10,9},{11,10},{13,12},{... | collective-permute-start | bytes 786440 | tf_op jit(solution)/shard_map/ppermute | solution.py:25
  32.9 9.7 %collective-permute-start.3 = (f32[2,2,4,16,256]{4,3,2,1,0:T(8,128)S(1)}, f32[2,2,4,16,256]{4,3,2,1,0:T(8,128)}, u32[]{:S(2)}, u32[]{:S(2)}) collective-permute-start(f32[2,2,4,16,256]{4,3,2,1,0:T(8,128)S(1)} %get-tuple-element.135), channel_id=1, source_target_pairs={{0,1},{1,2},{2,3},{4,5},{5,6},{6,7},{8,9},{9,10},{10,11},{12,13},{... | collective-permute-start | bytes 786440 | tf_op jit(solution)/shard_map/ppermute | solution.py:23
  66.2 9.0 %collective-permute-start.4 = (f32[2,2,4,16,256]{4,3,2,1,0:T(8,128)S(1)}, f32[2,2,4,16,256]{4,3,2,1,0:T(8,128)S(1)}, u32[]{:S(2)}, u32[]{:S(2)}) collective-permute-start(f32[2,2,4,16,256]{4,3,2,1,0:T(8,128)S(1)} %get-tuple-element.132), channel_id=1, source_target_pairs={{1,0},{2,1},{3,2},{5,4},{6,5},{7,6},{9,8},{10,9},{11,10},{13,12},{... | collective-permute-start | bytes 786440 | tf_op jit(solution)/shard_map/ppermute | solution.py:25
  67.5 9.0 %collective-permute-start.5 = (f32[2,2,4,16,256]{4,3,2,1,0:T(8,128)S(1)}, f32[2,2,4,16,256]{4,3,2,1,0:T(8,128)S(1)}, u32[]{:S(2)}, u32[]{:S(2)}) collective-permute-start(f32[2,2,4,16,256]{4,3,2,1,0:T(8,128)S(1)} %get-tuple-element.133), channel_id=1, source_target_pairs={{0,1},{1,2},{2,3},{4,5},{5,6},{6,7},{8,9},{9,10},{10,11},{12,13},{... | collective-permute-start | bytes 786440 | tf_op jit(solution)/shard_map/ppermute | solution.py:23
  89.8 11.7 %copy-start.6 = (f32[2,2,16,16,256]{4,3,2,1,0:T(8,128)S(1)}, f32[2,2,16,16,256]{4,3,2,1,0:T(8,128)}, u32[]{:S(2)}) copy-start(f32[2,2,16,16,256]{4,3,2,1,0:T(8,128)} %scatter-add.29) | copy-start | bytes 3145732
  91.3 8.7 %collective-permute-start.6 = (f32[2,2,4,16,256]{4,3,2,1,0:T(8,128)S(1)}, f32[2,2,4,16,256]{4,3,2,1,0:T(8,128)S(1)}, u32[]{:S(2)}, u32[]{:S(2)}) collective-permute-start(f32[2,2,4,16,256]{4,3,2,1,0:T(8,128)S(1)} %get-tuple-element.130), channel_id=1, source_target_pairs={{1,0},{2,1},{3,2},{5,4},{6,5},{7,6},{9,8},{10,9},{11,10},{13,12},{... | collective-permute-start | bytes 786440 | tf_op jit(solution)/shard_map/ppermute | solution.py:25
  92.6 8.9 %collective-permute-start.7 = (f32[2,2,4,16,256]{4,3,2,1,0:T(8,128)S(1)}, f32[2,2,4,16,256]{4,3,2,1,0:T(8,128)S(1)}, u32[]{:S(2)}, u32[]{:S(2)}) collective-permute-start(f32[2,2,4,16,256]{4,3,2,1,0:T(8,128)S(1)} %get-tuple-element.131), channel_id=1, source_target_pairs={{0,1},{1,2},{2,3},{4,5},{5,6},{6,7},{8,9},{9,10},{10,11},{12,13},{... | collective-permute-start | bytes 786440 | tf_op jit(solution)/shard_map/ppermute | solution.py:23
  114.9 11.7 %copy-start.1 = (f32[2,2,16,16,256]{4,3,2,1,0:T(8,128)S(1)}, f32[2,2,16,16,256]{4,3,2,1,0:T(8,128)}, u32[]{:S(2)}) copy-start(f32[2,2,16,16,256]{4,3,2,1,0:T(8,128)} %scatter-add.30) | copy-start | bytes 3145732
  116.4 8.7 %collective-permute-start.8 = (f32[2,2,4,16,256]{4,3,2,1,0:T(8,128)S(1)}, f32[2,2,4,16,256]{4,3,2,1,0:T(8,128)S(1)}, u32[]{:S(2)}, u32[]{:S(2)}) collective-permute-start(f32[2,2,4,16,256]{4,3,2,1,0:T(8,128)S(1)} %get-tuple-element.128), channel_id=1, source_target_pairs={{1,0},{2,1},{3,2},{5,4},{6,5},{7,6},{9,8},{10,9},{11,10},{13,12},{... | collective-permute-start | bytes 786440 | tf_op jit(solution)/shard_map/ppermute | solution.py:25
  117.7 8.9 %collective-permute-start.9 = (f32[2,2,4,16,256]{4,3,2,1,0:T(8,128)S(1)}, f32[2,2,4,16,256]{4,3,2,1,0:T(8,128)S(1)}, u32[]{:S(2)}, u32[]{:S(2)}) collective-permute-start(f32[2,2,4,16,256]{4,3,2,1,0:T(8,128)S(1)} %get-tuple-element.129), channel_id=1, source_target_pairs={{0,1},{1,2},{2,3},{4,5},{5,6},{6,7},{8,9},{9,10},{10,11},{12,13},{... | collective-permute-start | bytes 786440 | tf_op jit(solution)/shard_map/ppermute | solution.py:23
  139.9 11.7 %copy-start.2 = (f32[2,2,16,16,256]{4,3,2,1,0:T(8,128)S(1)}, f32[2,2,16,16,256]{4,3,2,1,0:T(8,128)}, u32[]{:S(2)}) copy-start(f32[2,2,16,16,256]{4,3,2,1,0:T(8,128)} %scatter-add.31) | copy-start | bytes 3145732
  141.4 8.7 %collective-permute-start.10 = (f32[2,2,4,16,256]{4,3,2,1,0:T(8,128)S(1)}, f32[2,2,4,16,256]{4,3,2,1,0:T(8,128)S(1)}, u32[]{:S(2)}, u32[]{:S(2)}) collective-permute-start(f32[2,2,4,16,256]{4,3,2,1,0:T(8,128)S(1)} %get-tuple-element.126), channel_id=1, source_target_pairs={{1,0},{2,1},{3,2},{5,4},{6,5},{7,6},{9,8},{10,9},{11,10},{13,12},{... | collective-permute-start | bytes 786440 | tf_op jit(solution)/shard_map/ppermute | solution.py:25
  142.7 8.9 %collective-permute-start.11 = (f32[2,2,4,16,256]{4,3,2,1,0:T(8,128)S(1)}, f32[2,2,4,16,256]{4,3,2,1,0:T(8,128)S(1)}, u32[]{:S(2)}, u32[]{:S(2)}) collective-permute-start(f32[2,2,4,16,256]{4,3,2,1,0:T(8,128)S(1)} %get-tuple-element.127), channel_id=1, source_target_pairs={{0,1},{1,2},{2,3},{4,5},{5,6},{6,7},{8,9},{9,10},{10,11},{12,13},{... | collective-permute-start | bytes 786440 | tf_op jit(solution)/shard_map/ppermute | solution.py:23
  165.0 11.7 %copy-start.3 = (f32[2,2,16,16,256]{4,3,2,1,0:T(8,128)S(1)}, f32[2,2,16,16,256]{4,3,2,1,0:T(8,128)}, u32[]{:S(2)}) copy-start(f32[2,2,16,16,256]{4,3,2,1,0:T(8,128)} %scatter-add.34) | copy-start | bytes 3145732
  166.5 8.7 %collective-permute-start.12 = (f32[2,2,4,16,256]{4,3,2,1,0:T(8,128)S(1)}, f32[2,2,4,16,256]{4,3,2,1,0:T(8,128)S(1)}, u32[]{:S(2)}, u32[]{:S(2)}) collective-permute-start(f32[2,2,4,16,256]{4,3,2,1,0:T(8,128)S(1)} %get-tuple-element.124), channel_id=1, source_target_pairs={{1,0},{2,1},{3,2},{5,4},{6,5},{7,6},{9,8},{10,9},{11,10},{13,12},{... | collective-permute-start | bytes 786440 | tf_op jit(solution)/shard_map/ppermute | solution.py:25
  167.8 8.9 %collective-permute-start.13 = (f32[2,2,4,16,256]{4,3,2,1,0:T(8,128)S(1)}, f32[2,2,4,16,256]{4,3,2,1,0:T(8,128)S(1)}, u32[]{:S(2)}, u32[]{:S(2)}) collective-permute-start(f32[2,2,4,16,256]{4,3,2,1,0:T(8,128)S(1)} %get-tuple-element.125), channel_id=1, source_target_pairs={{0,1},{1,2},{2,3},{4,5},{5,6},{6,7},{8,9},{9,10},{10,11},{12,13},{... | collective-permute-start | bytes 786440 | tf_op jit(solution)/shard_map/ppermute | solution.py:23
  190.0 11.7 %copy-start.4 = (f32[2,2,16,16,256]{4,3,2,1,0:T(8,128)S(1)}, f32[2,2,16,16,256]{4,3,2,1,0:T(8,128)}, u32[]{:S(2)}) copy-start(f32[2,2,16,16,256]{4,3,2,1,0:T(8,128)} %scatter-add.35) | copy-start | bytes 3145732
  191.5 8.7 %collective-permute-start.14 = (f32[2,2,4,16,256]{4,3,2,1,0:T(8,128)S(1)}, f32[2,2,4,16,256]{4,3,2,1,0:T(8,128)S(1)}, u32[]{:S(2)}, u32[]{:S(2)}) collective-permute-start(f32[2,2,4,16,256]{4,3,2,1,0:T(8,128)S(1)} %get-tuple-element.122), channel_id=1, source_target_pairs={{1,0},{2,1},{3,2},{5,4},{6,5},{7,6},{9,8},{10,9},{11,10},{13,12},{... | collective-permute-start | bytes 786440 | tf_op jit(solution)/shard_map/ppermute | solution.py:25
  192.8 8.9 %collective-permute-start.15 = (f32[2,2,4,16,256]{4,3,2,1,0:T(8,128)S(1)}, f32[2,2,4,16,256]{4,3,2,1,0:T(8,128)S(1)}, u32[]{:S(2)}, u32[]{:S(2)}) collective-permute-start(f32[2,2,4,16,256]{4,3,2,1,0:T(8,128)S(1)} %get-tuple-element.123), channel_id=1, source_target_pairs={{0,1},{1,2},{2,3},{4,5},{5,6},{6,7},{8,9},{9,10},{10,11},{12,13},{... | collective-permute-start | bytes 786440 | tf_op jit(solution)/shard_map/ppermute | solution.py:23
  (22 other events, 120.3 us)
Sparse Core Ops, SparseCore 0:
  217.6 37.3 all-gather.1
where the time goes:
time: 273 us; the launch traced here: 272 us
  local copies, waits for them, and re-layouts  80.7 us (30%)
  other arithmetic  59.1 us (22%)
  waiting for transfers between devices  57 us (21%)
  starting transfers between devices  52.5 us (19%)
  between operations  19.9 us (7%)
    scatter-add x8, local copies, waits for them, and re-layouts, body(): updated = updated.at[:, :, :, :, INJECT_Z].add(planes)  52.5 us
    add x8, other arithmetic, body(): updated = 2.0 * centre - before + courant_sq * laplace_rows(extended)  43.4 us
    ppermute x8, starting transfers between devices, extended_2(): lax.ppermute(tail, axis, [(i, (i + 1) % count) for i in range(ends)])  42 us
    all_gather x1, waiting for transfers between devices, body(): shard_piece = lax.all_gather(fields, 'shot', axis=1, tiled=True)  30.6 us
    ppermute x8, waiting for transfers between devices, extended_2(): lax.ppermute(head, axis, [((i + 1) % count, i) for i in range(ends)])  16.1 us
    another operation x16, local copies, waits for them, and re-layouts  11.3 us
    select_n x8, other arithmetic, body(): updated = jnp.where(inside[None, None, :, None, None], updated, 0.0)  11.2 us
    ppermute x8, starting transfers between devices, extended_2(): lax.ppermute(head, axis, [((i + 1) % count, i) for i in range(ends)])  10.5 us
  transfers between devices with their start and end apart: 17, of which 17 were waited for; matrix products, arithmetic and copies ran while one was open for 2% of the time, Pallas kernels for 0%

commit v1 on v0

v1 whole, which is shorter than its diff:
```python
import functools

import jax
import jax.numpy as jnp
from jax import lax
from jax.experimental import pallas as pl
from jax.experimental.pallas import tpu as pltpu
from jax.sharding import PartitionSpec as P

STEPS = 8
INJECT_Z = 4
REACH = 4
CHUNK = 4
LANES = 128
MESH = pl.DeviceIdType.MESH

stencil_weights = (-205.0 / 72.0, 8.0 / 5.0, -1.0 / 5.0, 8.0 / 315.0, -1.0 / 560.0)
side_weight = 1.0 / 16.0


def split_two(values):
    high = values.astype(jnp.bfloat16)
    low = (values - high.astype(jnp.float32)).astype(jnp.bfloat16)
    return high, low


def band(size, block):
    i = lax.broadcasted_iota(jnp.int32, (size, size), 0)
    j = lax.broadcasted_iota(jnp.int32, (size, size), 1)
    gap = jnp.abs(i - j)
    out = jnp.zeros((size, size), jnp.float32)
    for distance in range(1, REACH + 1):
        out = jnp.where(gap == distance, side_weight * stencil_weights[distance], out)
    if block < size:
        out = jnp.where(i // block == j // block, out, 0.0)
    return out


def dot(a, b):
    return jnp.dot(a, b, preferred_element_type=jnp.float32)


def kernel(
    source_now, source_prev, receiver_now, receiver_prev, courant, source_cell, wavelet,
    receiver_cell, traces, perm, image_out, source_out, receiver_out,
    buf, cbuf, mbuf, inject, trace_rows, z_hi, z_lo, y_hi, y_lo,
    part, send_a, recv_a, send_b, recv_b, image,
    load_sem, halo_send, halo_recv, a_send, a_recv, b_send, b_recv, out_sem,
):
    shots, rows, ny, nz = source_now.shape
    fields = 2 * shots
    cells = rows * ny
    offsets = perm.shape[0]
    half = offsets // 2
    slabs = lax.axis_size("slab")
    shot_devices = lax.axis_size("shot")
    per_device = offsets // shot_devices
    slab = lax.axis_index("slab")
    me = lax.axis_index("shot")
    has_low = slab > 0
    has_high = slab < slabs - 1
    near = me + 1 - 2 * (me % 2)
    far = (me + shot_devices // 2) % shot_devices
    near_far = (near + shot_devices // 2) % shot_devices

    barrier = pltpu.get_barrier_semaphore()

    @pl.when(has_low)
    def _():
        pl.semaphore_signal(barrier, inc=1, device_id={"slab": slab - 1}, device_id_type=MESH)

    @pl.when(has_high)
    def _():
        pl.semaphore_signal(barrier, inc=1, device_id={"slab": slab + 1}, device_id_type=MESH)

    pl.semaphore_signal(barrier, inc=1, device_id={"shot": near}, device_id_type=MESH)
    pl.semaphore_signal(barrier, inc=1, device_id={"shot": far}, device_id_type=MESH)

    body_rows = pl.ds(REACH, rows)
    loads = []
    for w in range(fields):
        now, before = ((source_now, source_prev), (receiver_now, receiver_prev))[w % 2]
        loads.append(pltpu.make_async_copy(now.at[w // 2], buf.at[0, w, body_rows], load_sem.at[2 * w]))
        loads.append(pltpu.make_async_copy(before.at[w // 2], buf.at[1, w, body_rows], load_sem.at[2 * w + 1]))
    loads.append(pltpu.make_async_copy(courant, cbuf, load_sem.at[2 * fields]))
    for load in loads:
        load.start()

    pl.semaphore_wait(barrier, 2 + has_low.astype(jnp.int32) + has_high.astype(jnp.int32))

    def to_low(source, p, w):
        return pltpu.make_async_remote_copy(
            src_ref=source, dst_ref=buf.at[p, w, pl.ds(REACH + rows, REACH)],
            send_sem=halo_send.at[w, 0], recv_sem=halo_recv.at[p, w, 1],
            device_id={"slab": slab - 1}, device_id_type=MESH)

    def to_high(source, p, w):
        return pltpu.make_async_remote_copy(
            src_ref=source, dst_ref=buf.at[p, w, pl.ds(0, REACH)],
            send_sem=halo_send.at[w, 1], recv_sem=halo_recv.at[p, w, 0],
            device_id={"slab": slab + 1}, device_id_type=MESH)

    def low_rows(p, w):
        return buf.at[p, w, pl.ds(REACH, REACH)]

    def high_rows(p, w):
        return buf.at[p, w, pl.ds(rows, REACH)]

    for w in range(fields):
        now = (source_now, receiver_now)[w % 2]

        @pl.when(has_low)
        def _():
            to_low(now.at[w // 2, pl.ds(0, REACH)], 0, w).start()

        @pl.when(has_high)
        def _():
            to_high(now.at[w // 2, pl.ds(rows - REACH, REACH)], 0, w).start()

    edge = jnp.zeros((REACH, ny, nz), jnp.float32)

    @pl.when(slab == 0)
    def _():
        for w in range(fields):
            for p in range(2):
                buf[p, w, 0:REACH] = edge

    @pl.when(slab == slabs - 1)
    def _():
        for w in range(fields):
            for p in range(2):
                buf[p, w, REACH + rows : 2 * REACH + rows] = edge

    z_hi[...], z_lo[...] = split_two(band(nz, nz))
    y_hi[...], y_lo[...] = split_two(band(cells, ny))

    first = slab * cells
    lane = lax.broadcasted_iota(jnp.int32, (1, LANES), 1)
    cell_lanes = lax.broadcasted_iota(jnp.int32, (cells, LANES), 0) + first
    trace_rows[...] = jnp.zeros(trace_rows.shape, jnp.float32)
    for s in range(shots):
        amplitude = jnp.zeros((1, LANES), jnp.float32)
        for t in range(STEPS):
            amplitude = jnp.where(lane == (INJECT_Z - t) % LANES, wavelet[t, s], amplitude)
        inject[2 * s] = jnp.where(cell_lanes == source_cell[s], amplitude, 0.0)
        receivers = receiver_cell.shape[1]
        positions = lax.broadcasted_iota(jnp.int32, (cells, receivers), 0) + first
        hot = jnp.where(positions == receiver_cell[pl.ds(s, 1), :], 1.0, 0.0).astype(jnp.bfloat16)
        for t in range(STEPS):
            trace_rows[pl.ds((INJECT_Z - t) % LANES, 1), :] = traces[t, pl.ds(s, 1), :]
        amounts = trace_rows[...]
        high, rest = split_two(amounts)
        left = amounts - high.astype(jnp.float32)
        rest, low = split_two(left)
        total = jnp.zeros((cells, LANES), jnp.float32)
        for piece in (low, rest, high):
            total = total + lax.dot_general(
                hot, piece, (((1,), (1,)), ((), ())), preferred_element_type=jnp.float32)
        inject[2 * s + 1] = total

    for load in loads:
        load.wait()

    at_depth = lax.broadcasted_iota(jnp.int32, (CHUNK, ny, LANES), 2) == INJECT_Z

    def side_terms(p, w):
        values = buf[p, w, REACH : REACH + rows].reshape(cells, nz)
        high, low = split_two(values)
        total = dot(low, z_hi[...]) + dot(high, z_lo[...]) + dot(high, z_hi[...])
        total = total + (dot(y_hi[...], low) + dot(y_lo[...], high) + dot(y_hi[...], high))
        mbuf[w] = total.reshape(rows, ny, nz)

    def advance(p, q, w, r):
        centre = buf[p, w, REACH + r : REACH + r + CHUNK]
        total = (1.0 + 2.0 * side_weight) * stencil_weights[0] * centre + mbuf[w, r : r + CHUNK]
        for k in range(1, REACH + 1):
            total = total + stencil_weights[k] * (
                buf[p, w, REACH + r + k : REACH + r + k + CHUNK]
                + buf[p, w, REACH + r - k : REACH + r - k + CHUNK])
        updated = 2.0 * centre - buf[q, w, REACH + r : REACH + r + CHUNK] + cbuf[r : r + CHUNK] * total
        here = pl.ds(r * ny, CHUNK * ny)
        plane = inject[w, here, :]
        added = jnp.where(at_depth, plane.reshape(CHUNK, ny, LANES), 0.0)
        buf[q, w, REACH + r : REACH + r + CHUNK, :, 0:LANES] = updated[:, :, 0:LANES] + added
        if nz > LANES:
            buf[q, w, REACH + r : REACH + r + CHUNK, :, LANES:nz] = updated[:, :, LANES:nz]
        inject[w, here, :] = pltpu.roll(plane, 1, 1)

    def wait_low(p, w):
        @pl.when(has_low)
        def _():
            to_high(high_rows(p, w), p, w).wait_recv()
            to_low(low_rows(p, w), p, w).wait_send()

    def wait_high(p, w):
        @pl.when(has_high)
        def _():
            to_low(low_rows(p, w), p, w).wait_recv()
            to_high(high_rows(p, w), p, w).wait_send()

    def step(t, carry):
        p = t % 2
        q = 1 - p
        for w in range(fields):
            side_terms(p, w)
            for r in range(REACH, rows - REACH, CHUNK):
                advance(p, q, w, r)
            wait_low(p, w)
            advance(p, q, w, 0)

            @pl.when(has_low)
            def _():
                to_low(low_rows(q, w), q, w).start()

            wait_high(p, w)
            advance(p, q, w, rows - CHUNK)

            @pl.when(has_high)
            def _():
                to_high(high_rows(q, w), q, w).start()
        return carry

    lax.fori_loop(0, STEPS - 1, step, 0)

    p = (STEPS - 1) % 2
    q = 1 - p
    y_index = lax.broadcasted_iota(jnp.int32, (CHUNK, ny, nz), 1)

    def copy_a(group, b):
        block = pl.ds(b * CHUNK, CHUNK)
        return pltpu.make_async_remote_copy(
            src_ref=send_a.at[group, :, block], dst_ref=recv_a.at[group, :, block],
            send_sem=a_send.at[group, b], recv_sem=a_recv.at[group, b],
            device_id={"shot": near}, device_id_type=MESH)

    def copy_b(b):
        block = pl.ds(b * CHUNK, CHUNK)
        return pltpu.make_async_remote_copy(
            src_ref=send_b.at[:, block], dst_ref=recv_b.at[:, block],
            send_sem=b_send.at[b], recv_sem=b_recv.at[b],
            device_id={"shot": far}, device_id_type=MESH)

    def correlate(b):
        r = b * CHUNK
        block = slice(REACH + r, REACH + r + CHUNK)
        for k in range(offsets):
            h = k - half
            total = None
            for s in range(shots):
                source = buf[q, 2 * s, block]
                receiver = buf[q, 2 * s + 1, block]
                if h % ny:
                    source = pltpu.roll(source, h % ny, 1)
                    receiver = pltpu.roll(receiver, (-h) % ny, 1)
                total = source * receiver if total is None else total + source * receiver
            if h:
                total = jnp.where((y_index >= abs(h)) & (y_index < ny - abs(h)), total, 0.0)
            part[k, r : r + CHUNK] = total
        for group, device in ((0, near_far), (1, near)):
            for j in range(per_device):
                send_a[group, j, r : r + CHUNK] = part[perm[device * per_device + j], r : r + CHUNK]
            copy_a(group, b).start()

    def relay(b):
        r = b * CHUNK
        copy_a(0, b).wait_recv()
        for j in range(per_device):
            send_b[j, r : r + CHUNK] = (
                part[perm[far * per_device + j], r : r + CHUNK] + recv_a[0, j, r : r + CHUNK])
        copy_b(b).start()

    def finish(b):
        r = b * CHUNK
        copy_a(1, b).wait_recv()
        copy_b(b).wait_recv()
        for j in range(per_device):
            image[j, r : r + CHUNK] = (
                part[perm[me * per_device + j], r : r + CHUNK]
                + recv_a[1, j, r : r + CHUNK] + recv_b[j, r : r + CHUNK])
        block = pl.ds(r, CHUNK)
        pltpu.make_async_copy(image.at[:, block], image_out.at[:, block], out_sem.at[b]).start()

    blocks = rows // CHUNK
    inner = list(range(1, blocks - 1))
    outer = [0, blocks - 1]
    for w in range(fields):
        side_terms(p, w)
        for b in inner:
            advance(p, q, w, b * CHUNK)
    for b in inner:
        correlate(b)
    for b in inner:
        relay(b)
    stores = []
    for w in range(fields):
        wait_low(p, w)
        advance(p, q, w, 0)
        wait_high(p, w)
        advance(p, q, w, rows - CHUNK)
        out = (source_out, receiver_out)[w % 2]
        stores.append(pltpu.make_async_copy(buf.at[q, w, body_rows], out.at[w // 2], out_sem.at[blocks + w]))
        stores[-1].start()
    for b in outer:
        correlate(b)
    for b in outer:
        relay(b)
    for b in inner + outer:
        finish(b)
    for b in range(blocks):
        copy_a(0, b).wait_send()
        copy_a(1, b).wait_send()
        copy_b(b).wait_send()
        block = pl.ds(b * CHUNK, CHUNK)
        pltpu.make_async_copy(image.at[:, block], image_out.at[:, block], out_sem.at[b]).wait()
    for store in stores:
        store.wait()


def body(
    source_now, source_prev, receiver_now, receiver_prev, courant_sq, source_cell, wavelet,
    receiver_cell, traces, offset_perm,
):
    shots, rows, ny, nz = source_now.shape
    fields = 2 * shots
    cells = rows * ny
    offsets = offset_perm.shape[0]
    per_device = offsets // lax.axis_size("shot")
    blocks = rows // CHUNK
    anywhere = pl.BlockSpec(memory_space=pl.ANY)
    vector = pl.BlockSpec(memory_space=pltpu.VMEM)
    scalar = pl.BlockSpec(memory_space=pltpu.SMEM)
    f32 = jnp.float32
    field = jax.ShapeDtypeStruct(source_now.shape, f32)
    images = jax.ShapeDtypeStruct((per_device, rows, ny, nz), f32)
    return pl.pallas_call(
        kernel,
        out_shape=(images, field, field),
        in_specs=[anywhere] * 5 + [scalar, scalar, vector, vector, scalar],
        out_specs=(anywhere,) * 3,
        scratch_shapes=[
            pltpu.VMEM((2, fields, rows + 2 * REACH, ny, nz), f32),
            pltpu.VMEM((rows, ny, nz), f32),
            pltpu.VMEM((fields, rows, ny, nz), f32),
            pltpu.VMEM((fields, cells, LANES), f32),
            pltpu.VMEM((LANES, receiver_cell.shape[1]), f32),
            pltpu.VMEM((nz, nz), jnp.bfloat16),
            pltpu.VMEM((nz, nz), jnp.bfloat16),
            pltpu.VMEM((cells, cells), jnp.bfloat16),
            pltpu.VMEM((cells, cells), jnp.bfloat16),
            pltpu.VMEM((offsets, rows, ny, nz), f32),
            pltpu.VMEM((2, per_device, rows, ny, nz), f32),
            pltpu.VMEM((2, per_device, rows, ny, nz), f32),
            pltpu.VMEM((per_device, rows, ny, nz), f32),
            pltpu.VMEM((per_device, rows, ny, nz), f32),
            pltpu.VMEM((per_device, rows, ny, nz), f32),
            pltpu.SemaphoreType.DMA((2 * fields + 1,)),
            pltpu.SemaphoreType.DMA((fields, 2)),
            pltpu.SemaphoreType.DMA((2, fields, 2)),
            pltpu.SemaphoreType.DMA((2, blocks)),
            pltpu.SemaphoreType.DMA((2, blocks)),
            pltpu.SemaphoreType.DMA((blocks,)),
            pltpu.SemaphoreType.DMA((blocks,)),
            pltpu.SemaphoreType.DMA((blocks + fields,)),
        ],
        compiler_params=pltpu.CompilerParams(
            collective_id=0, has_side_effects=True, vmem_limit_bytes=40 * 1024 * 1024
        ),
    )(
        source_now, source_prev, receiver_now, receiver_prev, courant_sq, source_cell, wavelet,
        receiver_cell, traces, offset_perm,
    )


def solution(mesh):
    field = P(("runs", "shot"), "slab", None, None)
    in_specs = (
        field, field, field, field,
        P(("runs", "slab"), None, None),
        P(("runs", "shot")),
        P(None, ("runs", "shot")),
        P(("runs", "shot"), None),
        P(None, ("runs", "shot"), None),
        P("runs"),
    )
    return jax.shard_map(body, mesh=mesh, in_specs=in_specs, out_specs=(field,) * 3, check_vma=False)
```

time: 273 us -> 72.6 us (0.27)
  local copies, waits for them, and re-layouts: 80.7 us -> 8.99 us
  Pallas kernels: 0 us -> 62.5 us
  other arithmetic: 59.1 us -> 0 us
  waiting for transfers between devices: 57 us -> 0 us
  starting transfers between devices: 52.5 us -> 0 us
  between operations: 19.9 us -> 0.68 us
    pallas_call x0 -> x1, Pallas kernels: none -> 62.5 us  [body(): pl.pallas_call(kernel, out_shape=(images, field, field), in_specs=[anywhe...]
    scatter-add x8 -> x0, local copies, waits for them, and re-layouts: 52.5 us -> none  [body(): updated = updated.at[:, :, :, :, INJECT_Z].add(planes)]
    ppermute x16 -> x0, starting transfers between devices: 52.4 us -> none  [the longest x8 42 us: extended_2(): lax.ppermute(tail, axis, [(i, (i + 1) % count) for i in range(ends)])]
    add x18 -> x0, other arithmetic: 43.6 us -> none  [the longest x8 43.4 us: body(): updated = 2.0 * centre - before + courant_sq * laplace_rows(extended)]
    all_gather x1 -> x0, waiting for transfers between devices: 30.6 us -> none  [body(): shard_piece = lax.all_gather(fields, 'shot', axis=1, tiled=True)]
    ppermute x16 -> x0, waiting for transfers between devices: 26.3 us -> none  [the longest x8 16.1 us: extended_2(): lax.ppermute(head, axis, [((i + 1) % count, i) for i in range(ends)])]
    another operation x26 -> x0, local copies, waits for them, and re-layouts: 14.6 us -> none
    select_n x8 -> x0, other arithmetic: 11.2 us -> none  [body(): updated = jnp.where(inside[None, None, :, None, None], updated, 0.0)]
  transfers between devices with their start and end apart: 17 -> 0, of which waited for: 17 -> 0; matrix products, arithmetic and copies ran while one was open for 2% -> 0% of each run, Pallas kernels for 0% -> 0%
where the time goes in v1:
time: 72.6 us; the launch traced here: 72.1 us
  Pallas kernels  62.5 us (86%)
  local copies, waits for them, and re-layouts  8.99 us (12%)
    pallas_call x1, Pallas kernels, body(): pl.pallas_call(kernel, out_shape=(images, field, field), in_specs=[anywhe...  62.5 us
    unnamed x22, local copies, waits for them, and re-layouts  8.99 us

profile of v1, /device:TPU:0, one launch (start us, length us, event | category | flops | bytes accessed | tf_op | source)
XLA Modules:
  0.0 72.1 jit_solution(714299052187822772)
XLA Ops:
  0.6 0.0 copy-start.8
  0.6 0.0 copy-start.6
  0.7 0.0 copy-start.7
  0.7 0.8 %copy.13.wavelet = f32[8,2]{1,0:T(8,128)S(1)} copy(f32[8,2]{0,1:T(2,128)} %param.16) | data formatting | bytes 128 | tf_op args[6]
  1.4 0.0 copy-done.8
  1.4 0.0 copy-done.6
  1.4 0.0 copy-done.7
  1.4 0.0 copy-start
  1.4 1.0 %copy-done = f32[2,16,16,256]{3,2,1,0:T(8,128)S(1)} copy-done((f32[2,16,16,256]{3,2,1,0:T(8,128)S(1)}, f32[2,16,16,256]{3,2,1,0:T(8,128)}, u32[]{:S(2)}) %copy-start) | copy-done | bytes 524312
  2.5 0.0 copy-start.1
  2.5 1.0 %copy-done.1 = f32[2,16,16,256]{3,2,1,0:T(8,128)S(1)} copy-done((f32[2,16,16,256]{3,2,1,0:T(8,128)S(1)}, f32[2,16,16,256]{3,2,1,0:T(8,128)}, u32[]{:S(2)}) %copy-start.1) | copy-done | bytes 524312
  3.5 0.0 copy-start.2
  3.5 1.0 %copy-done.2 = f32[2,16,16,256]{3,2,1,0:T(8,128)S(1)} copy-done((f32[2,16,16,256]{3,2,1,0:T(8,128)S(1)}, f32[2,16,16,256]{3,2,1,0:T(8,128)}, u32[]{:S(2)}) %copy-start.2) | copy-done | bytes 524312
  4.6 0.0 copy-start.3
  4.6 1.0 %copy-done.3 = f32[2,16,16,256]{3,2,1,0:T(8,128)S(1)} copy-done((f32[2,16,16,256]{3,2,1,0:T(8,128)S(1)}, f32[2,16,16,256]{3,2,1,0:T(8,128)}, u32[]{:S(2)}) %copy-start.3) | copy-done | bytes 524312
  5.6 0.0 copy-start.4
  5.6 0.9 %copy-done.4 = f32[16,16,256]{2,1,0:T(8,128)S(1)} copy-done((f32[16,16,256]{2,1,0:T(8,128)S(1)}, f32[16,16,256]{2,1,0:T(8,128)}, u32[]{:S(2)}) %copy-start.4) | copy-done | bytes 262168
  6.6 0.0 copy-start.5
  6.6 0.7 copy-done.5
  7.3 62.5 %shard_map.121 = (f32[2,16,16,256]{3,2,1,0:T(8,128)S(1)}, f32[2,16,16,256]{3,2,1,0:T(8,128)S(1)}, f32[2,16,16,256]{3,2,1,0:T(8,128)S(1)}) custom-call(f32[2,16,16,256]{3,2,1,0:T(8,128)S(1)} %copy-done, f32[2,16,16,256]{3,2,1,0:T(8,128)S(1)} %copy-done.1, f32[2,16,16,256]{3,2,1,0:T(8,128)S(1)} %copy-done.2, f32[2,16,16,256]{3,2,1,0:T(8,128)S(1)} %copy-done.3, ...), custom_call_target="tpu_custom_call" | custom-call | tf_op jit(solution)/shard_map/pallas_call | solution.py:335
  69.8 0.8 %copy.17 = f32[2,16,16,256]{3,2,1,0:T(8,128)} copy(f32[2,16,16,256]{3,2,1,0:T(8,128)S(1)} %get-tuple-element.6) | data formatting | bytes 1048576
  70.5 0.8 %copy.18 = f32[2,16,16,256]{3,2,1,0:T(8,128)} copy(f32[2,16,16,256]{3,2,1,0:T(8,128)S(1)} %get-tuple-element.7) | data formatting | bytes 1048576
  71.3 0.8 %copy.19 = f32[2,16,16,256]{3,2,1,0:T(8,128)} copy(f32[2,16,16,256]{3,2,1,0:T(8,128)S(1)} %get-tuple-element.8) | data formatting | bytes 1048576
Async XLA Ops:
  0.6 0.8 %copy-start.8 = (s32[8]{0:T(128)S(1)}, s32[8]{0:T(128)}, u32[]{:S(2)}) copy-start(s32[8]{0:T(128)} %perm.1) | copy-start | bytes 100
  0.6 0.8 %copy-start.6 = (s32[2,256]{1,0:T(2,128)S(1)}, s32[2,256]{1,0:T(2,128)}, u32[]{:S(2)}) copy-start(s32[2,256]{1,0:T(2,128)} %receiver_cell.1) | copy-start | bytes 6148
  0.7 0.8 %copy-start.7 = (s32[2]{0:T(128)S(1)}, s32[2]{0:T(128)}, u32[]{:S(2)}) copy-start(s32[2]{0:T(128)} %source_cell.1) | copy-start | bytes 28
  1.4 1.0 %copy-start = (f32[2,16,16,256]{3,2,1,0:T(8,128)S(1)}, f32[2,16,16,256]{3,2,1,0:T(8,128)}, u32[]{:S(2)}) copy-start(f32[2,16,16,256]{3,2,1,0:T(8,128)} %source_now.1) | copy-start | bytes 1572868
  2.5 1.0 %copy-start.1 = (f32[2,16,16,256]{3,2,1,0:T(8,128)S(1)}, f32[2,16,16,256]{3,2,1,0:T(8,128)}, u32[]{:S(2)}) copy-start(f32[2,16,16,256]{3,2,1,0:T(8,128)} %source_prev.1) | copy-start | bytes 1572868
  3.5 1.0 %copy-start.2 = (f32[2,16,16,256]{3,2,1,0:T(8,128)S(1)}, f32[2,16,16,256]{3,2,1,0:T(8,128)}, u32[]{:S(2)}) copy-start(f32[2,16,16,256]{3,2,1,0:T(8,128)} %receiver_now.1) | copy-start | bytes 1572868
  4.6 1.0 %copy-start.3 = (f32[2,16,16,256]{3,2,1,0:T(8,128)S(1)}, f32[2,16,16,256]{3,2,1,0:T(8,128)}, u32[]{:S(2)}) copy-start(f32[2,16,16,256]{3,2,1,0:T(8,128)} %receiver_prev.1) | copy-start | bytes 1572868
  5.6 0.9 %copy-start.4 = (f32[16,16,256]{2,1,0:T(8,128)S(1)}, f32[16,16,256]{2,1,0:T(8,128)}, u32[]{:S(2)}) copy-start(f32[16,16,256]{2,1,0:T(8,128)} %courant.1) | copy-start | bytes 786436
  6.6 0.7 copy-start.5

commit v2 on v1

--- a/solution.py
+++ b/solution.py
@@ -12,6 +12,7 @@
 REACH = 4
 CHUNK = 4
 LANES = 128
+GRANT = 62 * 1024 * 1024
 MESH = pl.DeviceIdType.MESH
 
 stencil_weights = (-205.0 / 72.0, 8.0 / 5.0, -1.0 / 5.0, 8.0 / 315.0, -1.0 / 560.0)
@@ -42,9 +43,9 @@
 
 def kernel(
     source_now, source_prev, receiver_now, receiver_prev, courant, source_cell, wavelet,
-    receiver_cell, traces, perm, image_out, source_out, receiver_out,
+    receiver_cell, traces_far, perm, image_out, source_out, receiver_out,
     buf, cbuf, mbuf, inject, trace_rows, z_hi, z_lo, y_hi, y_lo,
-    part, send_a, recv_a, send_b, recv_b, image,
+    part, send_a, recv_a, send_b, recv_b, image, traces,
     load_sem, halo_send, halo_recv, a_send, a_recv, b_send, b_recv, out_sem,
 ):
     shots, rows, ny, nz = source_now.shape
@@ -83,6 +84,8 @@
         loads.append(pltpu.make_async_copy(now.at[w // 2], buf.at[0, w, body_rows], load_sem.at[2 * w]))
         loads.append(pltpu.make_async_copy(before.at[w // 2], buf.at[1, w, body_rows], load_sem.at[2 * w + 1]))
     loads.append(pltpu.make_async_copy(courant, cbuf, load_sem.at[2 * fields]))
+    trace_load = pltpu.make_async_copy(traces_far, traces, load_sem.at[2 * fields + 1])
+    trace_load.start()
     for load in loads:
         load.start()
 
@@ -138,10 +141,11 @@
     lane = lax.broadcasted_iota(jnp.int32, (1, LANES), 1)
     cell_lanes = lax.broadcasted_iota(jnp.int32, (cells, LANES), 0) + first
     trace_rows[...] = jnp.zeros(trace_rows.shape, jnp.float32)
+    trace_load.wait()
     for s in range(shots):
         amplitude = jnp.zeros((1, LANES), jnp.float32)
         for t in range(STEPS):
-            amplitude = jnp.where(lane == (INJECT_Z - t) % LANES, wavelet[t, s], amplitude)
+            amplitude = jnp.where(lane == (INJECT_Z - t) % LANES, wavelet[s, t], amplitude)
         inject[2 * s] = jnp.where(cell_lanes == source_cell[s], amplitude, 0.0)
         receivers = receiver_cell.shape[1]
         positions = lax.broadcasted_iota(jnp.int32, (cells, receivers), 0) + first
@@ -316,6 +320,18 @@
         store.wait()
 
 
+def store_kernel(image, source, receiver, image_out, source_out, receiver_out, sem):
+    pairs = ((image, image_out), (source, source_out), (receiver, receiver_out))
+    copies = [
+        pltpu.make_async_copy(a.at[j], b.at[j], sem.at[i, j])
+        for i, (a, b) in enumerate(pairs) for j in range(a.shape[0])
+    ]
+    for copy in copies:
+        copy.start()
+    for copy in copies:
+        copy.wait()
+
+
 def body(
     source_now, source_prev, receiver_now, receiver_prev, courant_sq, source_cell, wavelet,
     receiver_cell, traces, offset_perm,
@@ -327,15 +343,16 @@
     per_device = offsets // lax.axis_size("shot")
     blocks = rows // CHUNK
     anywhere = pl.BlockSpec(memory_space=pl.ANY)
+    main = pl.BlockSpec(memory_space=pltpu.HBM)
     vector = pl.BlockSpec(memory_space=pltpu.VMEM)
     scalar = pl.BlockSpec(memory_space=pltpu.SMEM)
     f32 = jnp.float32
     field = jax.ShapeDtypeStruct(source_now.shape, f32)
     images = jax.ShapeDtypeStruct((per_device, rows, ny, nz), f32)
-    return pl.pallas_call(
+    results = pl.pallas_call(
         kernel,
         out_shape=(images, field, field),
-        in_specs=[anywhere] * 5 + [scalar, scalar, vector, vector, scalar],
+        in_specs=[main] * 5 + [scalar, scalar, vector, main, scalar],
         out_specs=(anywhere,) * 3,
         scratch_shapes=[
             pltpu.VMEM((2, fields, rows + 2 * REACH, ny, nz), f32),
@@ -353,7 +370,8 @@
             pltpu.VMEM((per_device, rows, ny, nz), f32),
             pltpu.VMEM((per_device, rows, ny, nz), f32),
             pltpu.VMEM((per_device, rows, ny, nz), f32),
-            pltpu.SemaphoreType.DMA((2 * fields + 1,)),
+            pltpu.VMEM(traces.shape, f32),
+            pltpu.SemaphoreType.DMA((2 * fields + 2,)),
             pltpu.SemaphoreType.DMA((fields, 2)),
             pltpu.SemaphoreType.DMA((2, fields, 2)),
             pltpu.SemaphoreType.DMA((2, blocks)),
@@ -363,12 +381,20 @@
             pltpu.SemaphoreType.DMA((blocks + fields,)),
         ],
         compiler_params=pltpu.CompilerParams(
-            collective_id=0, has_side_effects=True, vmem_limit_bytes=40 * 1024 * 1024
+            collective_id=0, has_side_effects=True, vmem_limit_bytes=GRANT
         ),
     )(
-        source_now, source_prev, receiver_now, receiver_prev, courant_sq, source_cell, wavelet,
+        source_now, source_prev, receiver_now, receiver_prev, courant_sq, source_cell, wavelet.T,
         receiver_cell, traces, offset_perm,
     )
+    return pl.pallas_call(
+        store_kernel,
+        out_shape=(images, field, field),
+        in_specs=[anywhere] * 3,
+        out_specs=(main,) * 3,
+        scratch_shapes=[pltpu.SemaphoreType.DMA((3, max(shots, per_device)))],
+        compiler_params=pltpu.CompilerParams(vmem_limit_bytes=GRANT),
+    )(*results)
 
 
 def solution(mesh):

time: 72.6 us -> 113 us (1.56)
  Pallas kernels: 62.5 us -> 112 us
  local copies, waits for them, and re-layouts: 8.99 us -> 0 us
    pallas_call x1 -> x2, Pallas kernels: 62.5 us -> 112 us  [the longest x1 63.5 us: body(): pl.pallas_call(kernel, out_shape=(images, field, field), in_specs=[main]...]
    unnamed x22 -> x0, local copies, waits for them, and re-layouts: 8.99 us -> none
where the time goes in v2:
time: 113 us
  Pallas kernels  112 us (99%)
    pallas_call x1, Pallas kernels, body(): pl.pallas_call(kernel, out_shape=(images, field, field), in_specs=[main]...  63.5 us
    pallas_call x1, Pallas kernels, body(): pl.pallas_call(store_kernel, out_shape=(images, field, field), in_specs=[...  48.8 us

profile of v2, /device:TPU:0, one launch (start us, length us, event | category | flops | bytes accessed | tf_op | source)
XLA Modules:
  0.0 112.9 jit_solution(6865765098273540535)
XLA Ops:
  0.6 63.5 %shard_map.121 = (f32[2,16,16,256]{3,2,1,0:T(8,128)}, f32[2,16,16,256]{3,2,1,0:T(8,128)}, f32[2,16,16,256]{3,2,1,0:T(8,128)}) custom-call(f32[2,16,16,256]{3,2,1,0:T(8,128)} %source_now.1, f32[2,16,16,256]{3,2,1,0:T(8,128)} %source_prev.1, f32[2,16,16,256]{3,2,1,0:T(8,128)} %receiver_now.1, f32[2,16,16,256]{3,2,1,0:T(8,128)} %receiver_prev.1, ...), custom_call_target="tpu_custom_call" | custom-call | tf_op jit(solution)/shard_map/pallas_call | solution.py:352
  64.1 48.8 %shard_map.122 = (f32[2,16,16,256]{3,2,1,0:T(8,128)}, f32[2,16,16,256]{3,2,1,0:T(8,128)}, f32[2,16,16,256]{3,2,1,0:T(8,128)}) custom-call(f32[2,16,16,256]{3,2,1,0:T(8,128)} %get-tuple-element.6.image, f32[2,16,16,256]{3,2,1,0:T(8,128)} %get-tuple-element.7.source, f32[2,16,16,256]{3,2,1,0:T(8,128)} %get-tuple-element.8.receiver), custom_call_target="tpu_custom_call" | custom-call | tf_op jit(solution)/shard_map/pallas_call | solution.py:390

commit v3 on v2

--- a/solution.py
+++ b/solution.py
@@ -320,16 +320,21 @@
         store.wait()
 
 
-def store_kernel(image, source, receiver, image_out, source_out, receiver_out, sem):
+def store_kernel(image, source, receiver, image_out, source_out, receiver_out, held, load_sem, store_sem):
     pairs = ((image, image_out), (source, source_out), (receiver, receiver_out))
-    copies = [
-        pltpu.make_async_copy(a.at[j], b.at[j], sem.at[i, j])
-        for i, (a, b) in enumerate(pairs) for j in range(a.shape[0])
-    ]
-    for copy in copies:
-        copy.start()
-    for copy in copies:
-        copy.wait()
+    moves = []
+    for i, (value, out) in enumerate(pairs):
+        for j in range(value.shape[0]):
+            load = pltpu.make_async_copy(value.at[j], held.at[i, j], load_sem.at[i, j])
+            store = pltpu.make_async_copy(held.at[i, j], out.at[j], store_sem.at[i, j])
+            moves.append((load, store))
+    for load, _ in moves:
+        load.start()
+    for load, store in moves:
+        load.wait()
+        store.start()
+    for _, store in moves:
+        store.wait()
 
 
 def body(
@@ -392,7 +397,11 @@
         out_shape=(images, field, field),
         in_specs=[anywhere] * 3,
         out_specs=(main,) * 3,
-        scratch_shapes=[pltpu.SemaphoreType.DMA((3, max(shots, per_device)))],
+        scratch_shapes=[
+            pltpu.VMEM((3, max(shots, per_device), rows, ny, nz), f32),
+            pltpu.SemaphoreType.DMA((3, max(shots, per_device))),
+            pltpu.SemaphoreType.DMA((3, max(shots, per_device))),
+        ],
         compiler_params=pltpu.CompilerParams(vmem_limit_bytes=GRANT),
     )(*results)
 

time: 113 us -> 66.5 us (0.59)
  Pallas kernels: 112 us -> 65.7 us
    pallas_call x1, Pallas kernels: 48.8 us -> 2.19 us  [body(): pl.pallas_call(store_kernel, out_shape=(images, field, field), in_specs=[...]
where the time goes in v3:
time: 66.5 us; the launch traced here: 66.3 us
  Pallas kernels  65.7 us (99%)
    pallas_call x1, Pallas kernels, body(): pl.pallas_call(kernel, out_shape=(images, field, field), in_specs=[main]...  63.5 us
    pallas_call x1, Pallas kernels, body(): pl.pallas_call(store_kernel, out_shape=(images, field, field), in_specs=[...  2.19 us

profile of v3, /device:TPU:0, one launch (start us, length us, event | category | flops | bytes accessed | tf_op | source)
XLA Modules:
  0.0 66.3 jit_solution(8458202305651096796)
XLA Ops:
  0.6 63.5 %shard_map.121 = (f32[2,16,16,256]{3,2,1,0:T(8,128)}, f32[2,16,16,256]{3,2,1,0:T(8,128)}, f32[2,16,16,256]{3,2,1,0:T(8,128)}) custom-call(f32[2,16,16,256]{3,2,1,0:T(8,128)} %source_now.1, f32[2,16,16,256]{3,2,1,0:T(8,128)} %source_prev.1, f32[2,16,16,256]{3,2,1,0:T(8,128)} %receiver_now.1, f32[2,16,16,256]{3,2,1,0:T(8,128)} %receiver_prev.1, ...), custom_call_target="tpu_custom_call" | custom-call | tf_op jit(solution)/shard_map/pallas_call | solution.py:357
  64.1 2.2 %shard_map.122 = (f32[2,16,16,256]{3,2,1,0:T(8,128)}, f32[2,16,16,256]{3,2,1,0:T(8,128)}, f32[2,16,16,256]{3,2,1,0:T(8,128)}) custom-call(f32[2,16,16,256]{3,2,1,0:T(8,128)} %get-tuple-element.6.image, f32[2,16,16,256]{3,2,1,0:T(8,128)} %get-tuple-element.7.source, f32[2,16,16,256]{3,2,1,0:T(8,128)} %get-tuple-element.8.receiver), custom_call_target="tpu_custom_call" | custom-call | tf_op jit(solution)/shard_map/pallas_call | solution.py:395
